TPU v7x, 128 devices: a whole 4x4x4 slice. The times are simulated.
128 devices in a mesh: wave: 32 (over z, y, core), lev: 4 (over x).
Axes of the slice: x: 4, y: 4, z: 4, core: 2. Of those that a mesh axis runs over, the one named last changes fastest.
Arguments:
- grid_adjoint: bfloat16 [3, 16, 128, 1536], P(None, 'lev', 'wave'), may hold values from -6 to 6
- courant: bfloat16 [16, 128, 1536], P('lev', 'wave'), may hold values from -0.8984375 to 0.8984375
- row_points: int32 [128], P('wave'), may hold values from 20 to 1536, as said below
- wave_order: int32 [512], replicated, may hold values from 0 to 511, as said below
- legendre: bfloat16 [512, 512, 128], P('wave', 'lev'), may hold values from -0.013671875 to 0.013671875
- vert_inverse: float32 [3, 16, 16], replicated, as said below
Outputs:
- spectral_adjoint: float32 [3, 16, 512, 2, 512], P(None, None, ('wave', 'lev'))
Inputs may be any that keep to these rules, and one draw needn't show every extreme that they name: Row j has row_points[j] grid points; positions at or beyond it are unused. `wave_order`: A permutation of the wavenumbers 0 to 511 in which slots 2 i and 2 i + 1 hold wavenumbers that sum to 511. `vert_inverse`: each field's matrix has diagonal entries between 0.5 and 2 plus a dense coupling of independent entries.
All inputs are finite; a program needn't handle non-finite values.
Results may differ from a plain program's by a relative error of at most 0.0047.
Values may be sent and summed in bfloat16 or wider, within the bound.
A program may use at most 64 MiB of HBM per device.

v0:
```python
import math

import jax
import jax.numpy as jnp
from jax import lax
from jax.sharding import PartitionSpec as P

TWO_PI = 2.0 * math.pi


def advect(grid_rows, wind_rows, points):
    row_width = grid_rows.shape[-1]
    positions = jnp.arange(row_width, dtype=jnp.int32)
    counts = points[:, None]
    inside = positions[None, :] < counts
    at_end = positions[None, :] == counts - 1
    mass_flux = jnp.where(
        inside, wind_rows.astype(jnp.float32)[None] * grid_rows.astype(jnp.float32), 0.0
    )
    first_flux = mass_flux[..., :1]
    last_flux = jnp.sum(jnp.where(at_end, mass_flux, 0.0), axis=-1, keepdims=True)
    forward_flux = jnp.where(at_end, first_flux, jnp.roll(mass_flux, -1, axis=-1))
    backward_flux = jnp.where(positions == 0, last_flux, jnp.roll(mass_flux, 1, axis=-1))
    result = jnp.where(
        inside, grid_rows.astype(jnp.float32) + 0.5 * (forward_flux - backward_flux), 0.0
    )
    return result.astype(jnp.bfloat16)


def fourier_table(points, orders, row_width):
    positions = jnp.arange(row_width, dtype=jnp.int32)
    counts = points[:, None, None]
    phase_index = orders[None, None, :] * positions[None, :, None] % counts
    angles = phase_index.astype(jnp.float32) * (TWO_PI / counts.astype(jnp.float32))
    highest = (counts - 1) // 2
    factor = jnp.where(
        orders[None, None, :] > highest, 0.0, jnp.where(orders[None, None, :] == 0, 1.0, 2.0)
    ).astype(jnp.float32)
    cosines = jnp.stack([jnp.cos(angles) * factor, -jnp.sin(angles) * factor], axis=-1)
    return cosines.reshape(points.shape[0], row_width, 2 * orders.shape[0]).astype(jnp.bfloat16)


def body(grid_adjoint, courant, row_points, wave_order, legendre, vert_inverse):
    fields, levels_dev, row_count, row_width = grid_adjoint.shape
    row_group = math.gcd(4, row_count)

    def row_block(start):
        advected = advect(grid_adjoint, courant, row_points)
        cosines = fourier_table(row_points, wave_order, row_width)
        return lax.dot_general(
            advected, cosines, (((3,), (1,)), ((2,), (0,))), preferred_element_type=jnp.float32
        )

    starts = jnp.arange(0, row_count, row_group, dtype=jnp.int32)
    fourier = lax.map(row_block, starts)
    fourier = fourier.reshape(row_count, fields, levels_dev, -1).astype(jnp.bfloat16)
    fourier = jnp.transpose(fourier, (2, 1, 3, 0))
    table_quarter = lax.all_to_all(legendre, "lev", split_axis=0, concat_axis=1, tiled=True)
    spectral = lax.all_to_all(
        lax.all_to_all(fourier, "wave", split_axis=2, concat_axis=3, tiled=True),
        "lev",
        split_axis=2,
        concat_axis=0,
        tiled=True,
    )
    slot_count = table_quarter.shape[0]
    wave_total = table_quarter.shape[1]
    first_slot = (
        lax.axis_index("wave") * lax.axis_size("lev") + lax.axis_index("lev")
    ) * slot_count
    orders = lax.dynamic_slice_in_dim(wave_order, first_slot, slot_count, 0)
    degrees = jnp.arange(wave_total, dtype=jnp.int32)
    masked = jnp.where(
        degrees[None, :, None] >= orders[:, None, None], table_quarter, jnp.zeros((), jnp.bfloat16)
    )
    levels = spectral.shape[0]
    flattened = spectral.reshape(levels * fields, slot_count, 2, spectral.shape[-1])
    partial_value = lax.dot_general(
        flattened, masked, (((3,), (2,)), ((1,), (0,))), preferred_element_type=jnp.float32
    )
    partial_value = partial_value.reshape(slot_count, levels, fields, 2, wave_total)
    return jnp.einsum(
        "fpl,ipfcn->flicn", vert_inverse, partial_value, precision=lax.Precision.HIGHEST
    )


def solution(mesh):
    return jax.shard_map(
        body,
        mesh=mesh,
        in_specs=(
            P(None, "lev", "wave", None),
            P("lev", "wave", None),
            P("wave"),
            P(),
            P("wave", "lev", None),
            P(),
        ),
        out_specs=P(None, None, ("wave", "lev"), None, None),
        check_vma=False,
    )
```

profile of v0, /device:TPU:1, one launch (start us, length us, event | category | flops | bytes accessed | tf_op | source)
XLA Modules:
  0.0 428.4 jit_solution(5386987861250383691)
XLA Ops:
  0.0 0.7 broadcast_add_fusion
  0.7 0.7 iota_compare_fusion
  1.4 0.8 convert_element_type.46
  2.2 1.0 fusion.22
  3.6 0.7 compare_select_fusion.2
  4.2 0.9 iota_multiply_fusion
  5.2 0.7 broadcast_compare_fusion
  5.9 0.7 convert_divide_fusion
  6.5 0.9 compare_select_fusion
  7.4 344.2 %multiply_convert_fusion.1 = (bf16[4,1536,512,1]{1,0,3,2:T(4,128)(2,1)S(1)}, bf16[4,1536,512,1]{1,0,3,2:T(4,128)(2,1)S(1)}) fusion(f32[4,512]{0,1:T(8,128)S(1)} %compare_select_fusion, f32[4]{0:T(128)S(1)} %convert_divide_fusion, pred[4]{0:T(512)(128)(4,1)S(1)} %broadcast_compare_fusion, s32[4]{0:T(128)S(1)} %get-tuple-element.32, ...), kind=kLoop, calls=%fused_computation.11 | loop fusion | flops 44040192 | bytes 15736868 | tf_op jit(solution)/shard_map/convert
  351.6 8.4 %pad_maximum_fusion = bf16[4,1536,512,2]{1,0,3,2:T(4,128)(2,1)S(1)} fusion(bf16[4,1536,512,1]{1,0,3,2:T(4,128)(2,1)S(1)} %get-tuple-element.16, bf16[4,1536,512,1]{1,0,3,2:T(4,128)(2,1)S(1)} %get-tuple-element.15), kind=kLoop, calls=%fused_computation.7 | loop fusion | flops 6291456 | bytes 25165824 | tf_op jit(solution)/shard_map/while/body/eval_jaxpr/stack | solution.py:39
  360.6 5.0 %fusion.16 = bf16[4,3,1024,4]{2,0,1,3:T(4,128)(2,1)S(1)} fusion(bf16[4,1536,1024,1]{1,0,2,3:T(4,128)(2,1)S(1)} %bitcast.35, bf16[3,4,4,1536]{3,2,1,0:T(4,128)(2,1)S(1)} %fusion.12), kind=kOutput, calls=%fused_computation.23 | convolution fusion | flops 151044096 | bytes 12828672 | tf_op jit(solution)/shard_map/while/body/eval_jaxpr/dot_general | solution.py:50
  365.6 2.9 copy.38
  368.5 6.2 %reshape.186 = bf16[32,2,768]{2,1,0:T(2,128)(2,1)S(1)} reshape(bf16[1024,3,4,4]{3,2,1,0:T(4,128)(2,1)S(1)} %bitcast.36) | data formatting | bytes 196608
  374.7 16.8 %all_to_all.51 = bf16[32,2,768]{2,1,0:T(2,128)(2,1)S(1)} all-to-all(bf16[32,2,768]{2,1,0:T(2,128)(2,1)S(1)} %reshape.186), channel_id=1, replica_groups=mesh['wave'=32,'lev'=4] {'wave'}, dimensions={0} | all-to-all | bytes 196608 | tf_op jit(solution)/shard_map/all_to_all | solution.py:60
  391.5 6.7 %reshape.187 = bf16[1024,3,4,4]{3,2,1,0:T(4,128)(2,1)S(1)} reshape(bf16[32,2,768]{2,1,0:T(2,128)(2,1)S(1)} %all_to_all.51) | data formatting | bytes 196608
  398.2 5.8 %copy.39 = bf16[4,3,32,32,4]{3,4,2,1,0:T(4,128)(2,1)} copy(bf16[4,3,32,32,4]{4,0,1,3,2:T(4,128)(2,1)S(1)} %bitcast.37) | data formatting | bytes 196608 | tf_op jit(solution)/shard_map/all_to_all | solution.py:60
  404.0 1.2 copy.40
  405.1 8.5 %all_to_all.52 = bf16[4,3,32,128]{3,0,1,2:T(4,128)(2,1)S(1)} all-to-all(bf16[4,3,32,128]{3,0,1,2:T(4,128)(2,1)S(1)} %copy.40), channel_id=1, replica_groups=mesh['wave'=32,'lev'=4] {'lev'}, dimensions={2} | all-to-all | bytes 196608 | tf_op jit(solution)/shard_map/all_to_all | solution.py:59
  413.6 3.7 all-to-all-start.2
  417.3 0.8 dynamic_slice.3
  418.2 6.3 %all-to-all-done.2 = bf16[16,128,128]{2,1,0:T(8,128)(2,1)S(1)} async-done(((bf16[16,128,128]{2,1,0:T(8,128)(2,1)}), bf16[16,128,128]{2,1,0:T(8,128)(2,1)S(1)}, u32[]{:S(2)}, u32[]{:S(2)}) %all-to-all-start.2) | async-done | bytes 524320 | tf_op jit(solution)/shard_map/all_to_all | solution.py:58
  425.8 0.9 convolution_bitcast_fusion
  426.6 1.5 copy.48
  (15 shorter events, 2.4 us)
Async XLA Ops:
  0.0 425.8 %copy-start = (f32[3,16,16]{2,1,0:T(8,128)S(1)}, f32[3,16,16]{2,1,0:T(8,128)}, u32[]{:S(2)}) copy-start(f32[3,16,16]{2,1,0:T(8,128)} %param.11) | copy-start | bytes 9220
  351.6 8.4 %copy-start.1 = (bf16[3,4,4,1536]{3,2,1,0:T(4,128)(2,1)S(1)}, bf16[3,4,4,1536]{3,2,1,0:T(4,128)(2,1)}, u32[]{:S(2)}) copy-start(bf16[3,4,4,1536]{3,2,1,0:T(4,128)(2,1)} %param.6) | copy-start | bytes 442372
  413.6 10.8 %all-to-all-start.2 = ((bf16[16,128,128]{2,1,0:T(8,128)(2,1)}), bf16[16,128,128]{2,1,0:T(8,128)(2,1)S(1)}, u32[]{:S(2)}, u32[]{:S(2)}) async-start(bf16[16,128,128]{2,1,0:T(8,128)(2,1)} %param.10), calls=%async_computation.2 | async-start | bytes 1048576 | tf_op jit(solution)/shard_map/all_to_all | solution.py:58
where the time goes:
time: 431 us; the launch traced here: 428 us
  other arithmetic  361 us (84%)
  local copies, waits for them, and re-layouts  26 us (6%)
  blocking collectives  25.3 us (6%)
  waiting for transfers between devices  6.29 us (1%)
  matrix products  6.12 us (1%)
    another operation x1, other arithmetic  344 us
    all_to_all x1, blocking collectives, body(): lax.all_to_all(fourier, 'wave', split_axis=2, concat_axis=3, tiled=True)  16.8 us
    unnamed x6, local copies, waits for them, and re-layouts  13 us
  transfers between devices with their start and end apart: 1, of which 1 were waited for; matrix products, arithmetic and copies ran while one was open for 0% of the time, Pallas kernels for 0%

commit v1 on v0

v1 whole, which is shorter than its diff:
```python
import functools

import jax
import jax.numpy as jnp
from jax import lax
from jax.experimental import pallas as pl
from jax.experimental.pallas import tpu as pltpu
from jax.sharding import PartitionSpec as P

F32 = jnp.float32
BF16 = jnp.bfloat16
MESH = pl.DeviceIdType.MESH
NT = (((1,), (1,)), ((), ()))

SIN_PI = (3.1415927410125732, -5.167712688446045, 2.5501632690429688,
          -0.5992521643638611, 0.08205024898052216, -0.007028118707239628)
COS_PI = (1.0, -4.934802055358887, 4.058709144592285,
          -1.3352118730545044, 0.2349366992712021, -0.024395223706960678)


def horner(coefficients, z):
    value = jnp.full(z.shape, coefficients[-1], F32)
    for c in coefficients[-2::-1]:
        value = value * z + c
    return value


def unit_circle(steps, orders, count):
    inverse = 1.0 / count
    product = steps * orders
    turns = jnp.floor(product * inverse + 0.5)
    x = (product - turns * count) * inverse
    z = x * x
    s = x * horner(SIN_PI, z)
    c = horner(COS_PI, z)
    return 1.0 - 2.0 * s * s, -2.0 * s * c


def iota(shape, axis):
    return lax.broadcasted_iota(jnp.int32, shape, axis)


def advect(grid_ref, wind_ref, points_ref, rows_ref):
    fields, levels, rows, width = grid_ref.shape
    row = iota((rows, width), 0)
    count = jnp.full((rows, width), points_ref[0], jnp.int32)
    for j in range(1, rows):
        count = jnp.where(row == j, points_ref[j], count)
    position = iota((rows, width), 1)
    inside = position < count
    at_end = position == count - 1
    at_start = position == 0
    for level in range(levels):
        wind = wind_ref[level].astype(F32)
        for field in range(fields):
            grid = grid_ref[field, level].astype(F32)
            flux = jnp.where(inside, wind * grid, 0.0)
            first = flux[:, :1]
            last = jnp.sum(jnp.where(at_end, flux, 0.0), axis=1, keepdims=True)
            forward = jnp.where(at_end, first, pltpu.roll(flux, width - 1, 1))
            backward = jnp.where(at_start, last, pltpu.roll(flux, 1, 1))
            result = jnp.where(inside, grid + 0.5 * (forward - backward), 0.0)
            at = rows * (field * levels + level)
            for k1 in range(width // 128):
                rows_ref[k1, at:at + rows, :] = result[:, 128 * k1:128 * (k1 + 1)]
    used = rows * fields * levels
    rows_ref[:, used:, :] = jnp.zeros((rows_ref.shape[0], rows_ref.shape[1] - used, 128), F32)


def column_orders(orders_ref):
    slots = orders_ref.shape[1]
    orders = orders_ref[...].astype(F32)
    high = jnp.floor(orders * 0.5)
    low = orders - 2.0 * high
    pick = (iota((slots, slots), 0) == 4 * (iota((slots, slots), 1) % 128)
            + iota((slots, slots), 1) // 128).astype(F32).astype(BF16)
    pair = jnp.concatenate([high, low, jnp.zeros((6, slots), F32)], axis=0).astype(BF16)
    moved = jnp.dot(pair, pick, preferred_element_type=F32)
    return 2.0 * moved[0:1] + moved[1:2]


def row_transform(j, points_ref, orders, rows_ref, pages_ref):
    blocks = rows_ref.shape[0]
    slots = orders.shape[1]
    count = jnp.full((1, slots), points_ref[j], jnp.int32).astype(F32)
    fine_cos, fine_sin = unit_circle(iota((16, 1), 0).astype(F32), orders, count)
    mid_cos, mid_sin = unit_circle(16.0 * iota((8, 1), 0).astype(F32), orders, count)
    far_cos, far_sin = unit_circle(128.0 * iota((16, 1), 0).astype(F32), orders, count)
    weight = jnp.where(2.0 * orders >= count, 0.0, jnp.where(orders == 0.0, 1.0, 2.0))
    far_cos = far_cos * weight
    far_sin = far_sin * weight
    left = jnp.concatenate(
        [rows_ref[k1, pl.ds(j, 16, stride=4), :] for k1 in range(blocks)], axis=0
    ).astype(BF16)
    stacked = []
    for i in range(slots // 128):
        own = slice(128 * i, 128 * (i + 1))
        c0, s0 = fine_cos[:, own], fine_sin[:, own]
        real, imag = [], []
        for b in range(8):
            c1, s1 = mid_cos[b:b + 1, own], mid_sin[b:b + 1, own]
            real.append(c1 * c0 - s1 * s0)
            imag.append(c1 * s0 + s1 * c0)
        table = jnp.concatenate(
            [jnp.concatenate(real, axis=0), jnp.concatenate(imag, axis=0)], axis=1
        ).astype(BF16)
        partial = jnp.dot(left, table, preferred_element_type=F32)
        total_real = jnp.zeros((16, 128), F32)
        total_imag = jnp.zeros((16, 128), F32)
        for k1 in range(blocks):
            u = partial[16 * k1:16 * (k1 + 1), :128]
            v = partial[16 * k1:16 * (k1 + 1), 128:]
            c2, s2 = far_cos[k1:k1 + 1, own], far_sin[k1:k1 + 1, own]
            total_real = total_real + (c2 * u - s2 * v)
            total_imag = total_imag + (c2 * v + s2 * u)
        stacked += [total_real, total_imag]
    pages_ref[pl.ds(128 * j, 128), :] = jnp.transpose(jnp.concatenate(stacked, axis=0))


def vertical_table(vert_ref):
    fields, levels, _ = vert_ref.shape
    spread = (iota((2 * levels, levels), 0) // 2 == iota((2 * levels, levels), 1)).astype(F32)
    rows = jnp.concatenate(
        [lax.dot_general(spread, vert_ref[f], NT, precision=lax.Precision.HIGHEST,
                         preferred_element_type=F32) for f in range(fields)], axis=0)
    column = iota((levels, 512), 1)
    pick = (iota((levels, 512), 0) == 4 * (column // 128) + column % 4).astype(F32)
    block = jnp.dot(rows, pick, precision=lax.Precision.HIGHEST, preferred_element_type=F32)
    shape = block.shape
    row, column = iota(shape, 0), iota(shape, 1)
    keep = (row // (2 * levels) == column // 4 % 4) & (row % 2 == column // 16 % 2)
    block = jnp.where(keep, block, 0.0)
    slot = column // 32 % 4
    return jnp.concatenate([jnp.where(slot == i, block, 0.0) for i in range(4)], axis=0)


def finish(first_slot, order_ref, vert, pages_ref, joined_ref, table_ref, out_ref):
    sources, rows, _ = pages_ref.shape
    for s in range(sources):
        joined_ref[rows * s:rows * (s + 1), :] = pages_ref[s].astype(F32)
    high = vert.astype(BF16)
    low = (vert - high.astype(F32)).astype(BF16)
    mixed = None
    for v in range(4):
        block = joined_ref[128 * v:128 * (v + 1), :].astype(BF16)
        own = slice(128 * v, 128 * (v + 1))
        for part in (high, low):
            term = lax.dot_general(part[:, own], block, NT, preferred_element_type=F32)
            mixed = term if mixed is None else mixed + term
    mixed_high = mixed.astype(BF16)
    mixed_low = (mixed - mixed_high.astype(F32)).astype(BF16)
    both = jnp.concatenate([mixed_high, mixed_low], axis=1)
    fields, levels = out_ref.shape[0], out_ref.shape[1]
    lines = fields * levels * 2
    for i in range(4):
        table = jnp.concatenate([table_ref[v, i] for v in range(4)], axis=0)
        table = jnp.concatenate([table, table], axis=1)
        summed = lax.dot_general(both[lines * i:lines * (i + 1)], table, NT,
                                 preferred_element_type=F32)
        degree = iota(summed.shape, 1)
        summed = jnp.where(degree >= order_ref[first_slot + i], summed, 0.0)
        for q in range(fields * levels):
            out_ref[q // levels, q % levels, i] = summed[2 * q:2 * q + 2]


def kernel(waves, levs, grid_ref, wind_ref, points_ref, order_ref, orders_ref, legendre_ref,
           vert_ref, out_ref, rows_ref, pages_ref, send_ref, recv_ref, joined_ref, table_ref,
           send_sem, recv_sem, table_send_sem, table_recv_sem, local_sem):
    w, v = lax.axis_index("wave"), lax.axis_index("lev")
    devices = waves * levs
    me = w * levs + v
    barrier = pltpu.get_barrier_semaphore()

    def greet(step, carry):
        d = lax.rem(me + step, devices)
        pl.semaphore_signal(barrier, inc=1, device_id=(d // levs, lax.rem(d, levs)),
                            device_id_type=MESH)
        return carry

    lax.fori_loop(1, devices, greet, 0)
    advect(grid_ref, wind_ref, points_ref, rows_ref)
    orders = column_orders(orders_ref)
    pl.semaphore_wait(barrier, devices - 1)

    own_table = pltpu.make_async_copy(
        legendre_ref.at[pl.ds(4 * v, 4)], table_ref.at[v], local_sem.at[0])
    own_table.start()
    table_copies = []
    for step in range(1, levs):
        u = lax.rem(v + step, levs)
        copy = pltpu.make_async_remote_copy(
            src_ref=legendre_ref.at[pl.ds(4 * u, 4)], dst_ref=table_ref.at[v],
            send_sem=table_send_sem.at[step - 1], recv_sem=table_recv_sem.at[step - 1],
            device_id=(w, u), device_id_type=MESH)
        copy.start()
        table_copies.append(copy)

    for j in range(4):
        row_transform(j, points_ref, orders, rows_ref, pages_ref)

    slot = waves * v + w

    def pack(d):
        send_ref[d] = pages_ref[pl.ds(d, 4, stride=128), :].astype(BF16)

    pack(me)
    own_page = pltpu.make_async_copy(send_ref.at[me], recv_ref.at[slot], local_sem.at[1])
    own_page.start()

    def send(step, carry):
        d = lax.rem(me + step, devices)
        pack(d)
        pltpu.make_async_remote_copy(
            src_ref=send_ref.at[d], dst_ref=recv_ref.at[slot], send_sem=send_sem,
            recv_sem=recv_sem, device_id=(d // levs, lax.rem(d, levs)), device_id_type=MESH,
        ).start()
        return carry

    lax.fori_loop(1, devices, send, 0)
    vert = vertical_table(vert_ref)
    own_table.wait()
    for copy in table_copies:
        copy.wait()
    own_page.wait()
    every = pltpu.make_async_remote_copy(
        src_ref=send_ref.at[pl.ds(0, devices - 1)], dst_ref=recv_ref.at[pl.ds(0, devices - 1)],
        send_sem=send_sem, recv_sem=recv_sem,
        device_id=(w, lax.rem(v + 1, levs)), device_id_type=MESH)
    every.wait_recv()
    every.wait_send()
    finish(4 * me, order_ref, vert, recv_ref, joined_ref, table_ref, out_ref)


def body(grid_adjoint, courant, row_points, wave_order, legendre, vert_inverse, *, waves, levs):
    fields, levels, rows, width = grid_adjoint.shape
    slots = legendre.shape[0] // levs
    degrees = legendre.shape[1] * levs
    devices = waves * levs
    vmem = pl.BlockSpec(memory_space=pltpu.VMEM)
    smem = pl.BlockSpec(memory_space=pltpu.SMEM)
    return pl.pallas_call(
        functools.partial(kernel, waves, levs),
        out_shape=jax.ShapeDtypeStruct((fields, levels * levs, slots, 2, degrees), F32),
        in_specs=[vmem, vmem, smem, smem, vmem, pl.BlockSpec(memory_space=pl.ANY), vmem],
        out_specs=vmem,
        scratch_shapes=[
            pltpu.VMEM((width // 128, 64, 128), F32),
            pltpu.VMEM((rows * 128, 128), F32),
            pltpu.VMEM((devices, 4, 128), BF16),
            pltpu.VMEM((devices, 4, 128), BF16),
            pltpu.VMEM((512, 128), F32),
            pltpu.VMEM((levs, slots) + legendre.shape[1:], BF16),
            pltpu.SemaphoreType.DMA,
            pltpu.SemaphoreType.DMA,
            pltpu.SemaphoreType.DMA((levs - 1,)),
            pltpu.SemaphoreType.DMA((levs - 1,)),
            pltpu.SemaphoreType.DMA((2,)),
        ],
        compiler_params=pltpu.CompilerParams(
            collective_id=0, has_side_effects=True, vmem_limit_bytes=40 * 2**20),
    )(grid_adjoint, courant, row_points, wave_order, wave_order.reshape(1, -1), legendre,
      vert_inverse)


def solution(mesh):
    return jax.shard_map(
        functools.partial(body, waves=mesh.shape["wave"], levs=mesh.shape["lev"]),
        mesh=mesh,
        in_specs=(
            P(None, "lev", "wave", None),
            P("lev", "wave", None),
            P("wave"),
            P(),
            P("wave", "lev", None),
            P(),
        ),
        out_specs=P(None, None, ("wave", "lev"), None, None),
        check_vma=False,
    )
```

time: 431 us -> 30.8 us (0.07)
  other arithmetic: 361 us -> 0 us
  blocking collectives: 25.3 us -> 0 us
  Pallas kernels: 0 us -> 24.7 us
  local copies, waits for them, and re-layouts: 26 us -> 5.7 us
  waiting for transfers between devices: 6.29 us -> 0 us
  matrix products: 6.12 us -> 0 us
    another operation x2 -> x0, other arithmetic: 353 us -> none
    all_to_all x2 -> x0, blocking collectives: 25.3 us -> none  [the longest x1 16.8 us: body(): lax.all_to_all(fourier, 'wave', split_axis=2, concat_axis=3, tiled=True)]
    pallas_call x0 -> x1, Pallas kernels: none -> 24.7 us  [body(): pl.pallas_call(functools.partial(kernel, waves, levs), out_shape=jax.Shap...]
    unnamed x6 -> x13, local copies, waits for them, and re-layouts: 13 us -> 5.7 us
    all_to_all x5 -> x0, local copies, waits for them, and re-layouts: 6.99 us -> none  [the longest x2 6.92 us: body(): lax.all_to_all(fourier, 'wave', split_axis=2, concat_axis=3, tiled=True)]
    all_to_all x1 -> x0, waiting for transfers between devices: 6.29 us -> none  [body(): lax.all_to_all(legendre, 'lev', split_axis=0, concat_axis=1, tiled=True)]
    dot_general x3 -> x0, matrix products: 6.12 us -> none  [the longest x1 4.95 us: row_block(): lax.dot_general(advected, cosines, (((3,), (1,)), ((2,), (0,))), preferre...]
  transfers between devices with their start and end apart: 1 -> 0, of which waited for: 1 -> 0; matrix products, arithmetic and copies ran while one was open for 0% -> 0% of each run, Pallas kernels for 0% -> 0%
where the time goes in v1:
time: 30.8 us; the launch traced here: 30.4 us
  Pallas kernels  24.7 us (80%)
  local copies, waits for them, and re-layouts  5.7 us (19%)
    pallas_call x1, Pallas kernels, body(): pl.pallas_call(functools.partial(kernel, waves, levs), out_shape=jax.Shap...  24.7 us
    unnamed x13, local copies, waits for them, and re-layouts  5.7 us

profile of v1, /device:TPU:1, one launch (start us, length us, event | category | flops | bytes accessed | tf_op | source)
XLA Modules:
  0.0 30.4 jit_solution(4909305199295207121)
XLA Ops:
  0.0 0.0 copy-start.5
  0.0 0.7 %copy-done.5 = s32[4]{0:T(128)S(1)} copy-done((s32[4]{0:T(128)S(1)}, s32[4]{0:T(128)}, u32[]{:S(2)}) %copy-start.5) | copy-done | bytes 40
  0.7 0.0 copy-start
  0.7 1.0 %copy-done = bf16[16,128,128]{2,1,0:T(8,128)(2,1)S(1)} copy-done((bf16[16,128,128]{2,1,0:T(8,128)(2,1)S(1)}, bf16[16,128,128]{2,1,0:T(8,128)(2,1)}, u32[]{:S(2)}) %copy-start) | copy-done | bytes 524312
  1.7 0.0 copy-start.1
  1.7 0.9 %copy-done.1 = bf16[3,4,4,1536]{3,2,1,0:T(4,128)(2,1)S(1)} copy-done((bf16[3,4,4,1536]{3,2,1,0:T(4,128)(2,1)S(1)}, bf16[3,4,4,1536]{3,2,1,0:T(4,128)(2,1)}, u32[]{:S(2)}) %copy-start.1) | copy-done | bytes 147480
  2.6 0.0 copy-start.2
  2.6 0.8 %copy-done.2 = bf16[4,4,1536]{2,1,0:T(4,128)(2,1)S(1)} copy-done((bf16[4,4,1536]{2,1,0:T(4,128)(2,1)S(1)}, bf16[4,4,1536]{2,1,0:T(4,128)(2,1)}, u32[]{:S(2)}) %copy-start.2) | copy-done | bytes 49176
  3.4 0.0 copy-start.3
  3.4 0.7 %copy-done.3 = f32[3,16,16]{2,1,0:T(8,128)S(1)} copy-done((f32[3,16,16]{2,1,0:T(8,128)S(1)}, f32[3,16,16]{2,1,0:T(8,128)}, u32[]{:S(2)}) %copy-start.3) | copy-done | bytes 3096
  4.1 0.0 copy-start.4
  4.1 0.7 %copy-done.4 = s32[512]{0:T(512)S(1)} copy-done((s32[512]{0:T(512)S(1)}, s32[512]{0:T(512)}, u32[]{:S(2)}) %copy-start.4) | copy-done | bytes 2072
  4.8 24.7 %shard_map.64 = f32[3,16,4,2,512]{4,3,2,1,0:T(2,128)S(1)} custom-call(bf16[3,4,4,1536]{3,2,1,0:T(4,128)(2,1)S(1)} %copy-done.1, bf16[4,4,1536]{2,1,0:T(4,128)(2,1)S(1)} %copy-done.2, s32[4]{0:T(128)S(1)} %copy-done.5, s32[512]{0:T(512)S(1)} %copy-done.4, s32[1,512]{1,0:T(1,128)S(1)} %bitcast.1, bf16[16,128,128]{2,1,0:T(8,128)(2,1)S(1)} %copy-done, ...), custom_call_target="tpu_custom_call" | custom-call | tf_op jit(solution)/shard_map/pallas_call | solution.py:241
  29.6 0.9 %copy.8 = f32[3,16,4,2,512]{4,3,2,1,0:T(2,128)} copy(f32[3,16,4,2,512]{4,3,2,1,0:T(2,128)S(1)} %shard_map.64) | data formatting | bytes 1572864
Async XLA Ops:
  0.0 0.7 %copy-start.5 = (s32[4]{0:T(128)S(1)}, s32[4]{0:T(128)}, u32[]{:S(2)}) copy-start(s32[4]{0:T(128)} %points_ref.1) | copy-start | bytes 52
  0.7 1.0 %copy-start = (bf16[16,128,128]{2,1,0:T(8,128)(2,1)S(1)}, bf16[16,128,128]{2,1,0:T(8,128)(2,1)}, u32[]{:S(2)}) copy-start(bf16[16,128,128]{2,1,0:T(8,128)(2,1)} %legendre_ref.1) | copy-start | bytes 1572868
  1.7 0.9 %copy-start.1 = (bf16[3,4,4,1536]{3,2,1,0:T(4,128)(2,1)S(1)}, bf16[3,4,4,1536]{3,2,1,0:T(4,128)(2,1)}, u32[]{:S(2)}) copy-start(bf16[3,4,4,1536]{3,2,1,0:T(4,128)(2,1)} %grid_ref.1) | copy-start | bytes 442372
  2.6 0.8 %copy-start.2 = (bf16[4,4,1536]{2,1,0:T(4,128)(2,1)S(1)}, bf16[4,4,1536]{2,1,0:T(4,128)(2,1)}, u32[]{:S(2)}) copy-start(bf16[4,4,1536]{2,1,0:T(4,128)(2,1)} %wind_ref.1) | copy-start | bytes 147460
  3.4 0.7 %copy-start.3 = (f32[3,16,16]{2,1,0:T(8,128)S(1)}, f32[3,16,16]{2,1,0:T(8,128)}, u32[]{:S(2)}) copy-start(f32[3,16,16]{2,1,0:T(8,128)} %vert_ref.1) | copy-start | bytes 9220
  4.1 0.7 %copy-start.4 = (s32[512]{0:T(512)S(1)}, s32[512]{0:T(512)}, u32[]{:S(2)}) copy-start(s32[512]{0:T(512)} %order_ref.1) | copy-start | bytes 6148

commit v2 on v1

--- a/solution.py
+++ b/solution.py
@@ -42,18 +42,24 @@
 
 def advect(grid_ref, wind_ref, points_ref, rows_ref):
     fields, levels, rows, width = grid_ref.shape
-    row = iota((rows, width), 0)
-    count = jnp.full((rows, width), points_ref[0], jnp.int32)
+    shape = (2 * rows, width)
+    row = iota(shape, 0) % rows
+    count = jnp.full(shape, points_ref[0], jnp.int32)
     for j in range(1, rows):
         count = jnp.where(row == j, points_ref[j], count)
-    position = iota((rows, width), 1)
+    position = iota(shape, 1)
     inside = position < count
     at_end = position == count - 1
     at_start = position == 0
-    for level in range(levels):
-        wind = wind_ref[level].astype(F32)
+
+    def pair(ref, *at):
+        return jnp.concatenate(
+            [ref[(*at[:-1], at[-1] + half)].astype(F32) for half in range(2)], axis=0)
+
+    for level in range(0, levels, 2):
+        wind = pair(wind_ref, level)
         for field in range(fields):
-            grid = grid_ref[field, level].astype(F32)
+            grid = pair(grid_ref, field, level)
             flux = jnp.where(inside, wind * grid, 0.0)
             first = flux[:, :1]
             last = jnp.sum(jnp.where(at_end, flux, 0.0), axis=1, keepdims=True)
@@ -62,7 +68,7 @@
             result = jnp.where(inside, grid + 0.5 * (forward - backward), 0.0)
             at = rows * (field * levels + level)
             for k1 in range(width // 128):
-                rows_ref[k1, at:at + rows, :] = result[:, 128 * k1:128 * (k1 + 1)]
+                rows_ref[k1, at:at + 2 * rows, :] = result[:, 128 * k1:128 * (k1 + 1)]
     used = rows * fields * levels
     rows_ref[:, used:, :] = jnp.zeros((rows_ref.shape[0], rows_ref.shape[1] - used, 128), F32)
 
@@ -114,7 +120,7 @@
             total_real = total_real + (c2 * u - s2 * v)
             total_imag = total_imag + (c2 * v + s2 * u)
         stacked += [total_real, total_imag]
-    pages_ref[pl.ds(128 * j, 128), :] = jnp.transpose(jnp.concatenate(stacked, axis=0))
+    pages_ref[:, j, :] = jnp.transpose(jnp.concatenate(stacked, axis=0))
 
 
 def vertical_table(vert_ref):
@@ -135,9 +141,9 @@
 
 
 def finish(first_slot, order_ref, vert, pages_ref, joined_ref, table_ref, out_ref):
-    sources, rows, _ = pages_ref.shape
-    for s in range(sources):
-        joined_ref[rows * s:rows * (s + 1), :] = pages_ref[s].astype(F32)
+    levs, waves, rows, _ = pages_ref.shape
+    for s in range(levs * waves):
+        joined_ref[rows * s:rows * (s + 1), :] = pages_ref[s // waves, s % waves].astype(F32)
     high = vert.astype(BF16)
     low = (vert - high.astype(F32)).astype(BF16)
     mixed = None
@@ -163,30 +169,43 @@
             out_ref[q // levels, q % levels, i] = summed[2 * q:2 * q + 2]
 
 
-def kernel(waves, levs, grid_ref, wind_ref, points_ref, order_ref, orders_ref, legendre_ref,
-           vert_ref, out_ref, rows_ref, pages_ref, send_ref, recv_ref, joined_ref, table_ref,
-           send_sem, recv_sem, table_send_sem, table_recv_sem, local_sem):
+def kernel(waves, levs, grid_hbm, wind_hbm, points_hbm, order_hbm, orders_hbm, legendre_ref,
+           vert_hbm, out_ref, grid_ref, wind_ref, points_ref, order_ref, orders_ref, vert_ref,
+           rows_ref, pages_ref, send_ref, middle_ref, recv_ref, joined_ref, table_ref,
+           fetch_sem, wave_send_sem, wave_recv_sem, lev_send_sem, lev_recv_sem, table_send_sem,
+           table_recv_sem, local_sem):
     w, v = lax.axis_index("wave"), lax.axis_index("lev")
-    devices = waves * levs
     me = w * levs + v
-    barrier = pltpu.get_barrier_semaphore()
-
-    def greet(step, carry):
-        d = lax.rem(me + step, devices)
-        pl.semaphore_signal(barrier, inc=1, device_id=(d // levs, lax.rem(d, levs)),
-                            device_id_type=MESH)
-        return carry
-
-    lax.fori_loop(1, devices, greet, 0)
-    advect(grid_ref, wind_ref, points_ref, rows_ref)
-    orders = column_orders(orders_ref)
-    pl.semaphore_wait(barrier, devices - 1)
-
+    fetches = [
+        pltpu.make_async_copy(source, target, fetch_sem.at[at])
+        for at, (source, target) in enumerate((
+            (grid_hbm, grid_ref), (wind_hbm, wind_ref), (points_hbm, points_ref),
+            (order_hbm, order_ref), (orders_hbm, orders_ref), (vert_hbm, vert_ref)))
+    ]
+    for fetch in fetches:
+        fetch.start()
     own_table = pltpu.make_async_copy(
         legendre_ref.at[pl.ds(4 * v, 4)], table_ref.at[v], local_sem.at[0])
     own_table.start()
+
+    barrier = pltpu.get_barrier_semaphore()
+    for step in range(1, levs):
+        pl.semaphore_signal(barrier, inc=1, device_id=(w, lax.rem(v + step, levs)),
+                            device_id_type=MESH)
+
+    def greet(step, carry):
+        pl.semaphore_signal(barrier, inc=1, device_id=(lax.rem(w + step, waves), v),
+                            device_id_type=MESH)
+        return carry
+
+    lax.fori_loop(1, waves, greet, 0)
+    for fetch in fetches:
+        fetch.wait()
+    orders = column_orders(orders_ref)
+    pl.semaphore_wait(barrier, waves - 1 + levs - 1)
+
     table_copies = []
-    for step in range(1, levs):
+    for step in (2, 1, 3):
         u = lax.rem(v + step, levs)
         copy = pltpu.make_async_remote_copy(
             src_ref=legendre_ref.at[pl.ds(4 * u, 4)], dst_ref=table_ref.at[v],
@@ -195,39 +214,49 @@
         copy.start()
         table_copies.append(copy)
 
+    advect(grid_ref, wind_ref, points_ref, rows_ref)
     for j in range(4):
         row_transform(j, points_ref, orders, rows_ref, pages_ref)
-
-    slot = waves * v + w
-
-    def pack(d):
-        send_ref[d] = pages_ref[pl.ds(d, 4, stride=128), :].astype(BF16)
-
-    pack(me)
-    own_page = pltpu.make_async_copy(send_ref.at[me], recv_ref.at[slot], local_sem.at[1])
-    own_page.start()
+    send_ref[...] = pages_ref[...].astype(BF16).reshape(send_ref.shape)
 
     def send(step, carry):
-        d = lax.rem(me + step, devices)
-        pack(d)
+        target = lax.rem(w + step, waves)
         pltpu.make_async_remote_copy(
-            src_ref=send_ref.at[d], dst_ref=recv_ref.at[slot], send_sem=send_sem,
-            recv_sem=recv_sem, device_id=(d // levs, lax.rem(d, levs)), device_id_type=MESH,
+            src_ref=send_ref.at[target], dst_ref=middle_ref.at[:, w], send_sem=wave_send_sem,
+            recv_sem=wave_recv_sem, device_id=(target, v), device_id_type=MESH,
         ).start()
         return carry
 
-    lax.fori_loop(1, devices, send, 0)
+    lax.fori_loop(1, waves, send, 0)
+    own_pages = pltpu.make_async_copy(send_ref.at[w], middle_ref.at[:, w], local_sem.at[1])
+    own_pages.start()
     vert = vertical_table(vert_ref)
+    own_pages.wait()
+    partner = {"device_id": (lax.rem(w + 1, waves), v), "device_id_type": MESH}
+    arrived = middle_ref.at[:, pl.ds(0, waves - 1)]
+    pltpu.make_async_remote_copy(
+        src_ref=arrived, dst_ref=arrived, send_sem=wave_send_sem, recv_sem=wave_recv_sem,
+        **partner).wait_recv()
+
+    lev_copies = []
+    for step in (2, 1, 3):
+        u = lax.rem(v + step, levs)
+        copy = pltpu.make_async_remote_copy(
+            src_ref=middle_ref.at[u], dst_ref=recv_ref.at[v],
+            send_sem=lev_send_sem.at[step - 1], recv_sem=lev_recv_sem.at[step - 1],
+            device_id=(w, u), device_id_type=MESH)
+        copy.start()
+        lev_copies.append(copy)
+    own_block = pltpu.make_async_copy(middle_ref.at[v], recv_ref.at[v], local_sem.at[2])
+    own_block.start()
+    left = send_ref.at[pl.ds(0, waves - 1)]
+    pltpu.make_async_remote_copy(
+        src_ref=left, dst_ref=left, send_sem=wave_send_sem, recv_sem=wave_recv_sem,
+        **partner).wait_send()
+    own_block.wait()
     own_table.wait()
-    for copy in table_copies:
+    for copy in table_copies + lev_copies:
         copy.wait()
-    own_page.wait()
-    every = pltpu.make_async_remote_copy(
-        src_ref=send_ref.at[pl.ds(0, devices - 1)], dst_ref=recv_ref.at[pl.ds(0, devices - 1)],
-        send_sem=send_sem, recv_sem=recv_sem,
-        device_id=(w, lax.rem(v + 1, levs)), device_id_type=MESH)
-    every.wait_recv()
-    every.wait_send()
     finish(4 * me, order_ref, vert, recv_ref, joined_ref, table_ref, out_ref)
 
 
@@ -235,31 +264,39 @@
     fields, levels, rows, width = grid_adjoint.shape
     slots = legendre.shape[0] // levs
     degrees = legendre.shape[1] * levs
-    devices = waves * levs
-    vmem = pl.BlockSpec(memory_space=pltpu.VMEM)
-    smem = pl.BlockSpec(memory_space=pltpu.SMEM)
+    orders = wave_order.reshape(1, -1)
+    hbm = pl.BlockSpec(memory_space=pltpu.HBM)
     return pl.pallas_call(
         functools.partial(kernel, waves, levs),
         out_shape=jax.ShapeDtypeStruct((fields, levels * levs, slots, 2, degrees), F32),
-        in_specs=[vmem, vmem, smem, smem, vmem, pl.BlockSpec(memory_space=pl.ANY), vmem],
-        out_specs=vmem,
+        in_specs=[hbm] * 7,
+        out_specs=pl.BlockSpec(memory_space=pltpu.VMEM),
         scratch_shapes=[
+            pltpu.VMEM(grid_adjoint.shape, BF16),
+            pltpu.VMEM(courant.shape, BF16),
+            pltpu.SMEM(row_points.shape, jnp.int32),
+            pltpu.SMEM(wave_order.shape, jnp.int32),
+            pltpu.VMEM(orders.shape, jnp.int32),
+            pltpu.VMEM(vert_inverse.shape, F32),
             pltpu.VMEM((width // 128, 64, 128), F32),
-            pltpu.VMEM((rows * 128, 128), F32),
-            pltpu.VMEM((devices, 4, 128), BF16),
-            pltpu.VMEM((devices, 4, 128), BF16),
-            pltpu.VMEM((512, 128), F32),
+            pltpu.VMEM((waves * levs, rows, 128), F32),
+            pltpu.VMEM((waves, levs, rows, 128), BF16),
+            pltpu.VMEM((levs, waves, rows, 128), BF16),
+            pltpu.VMEM((levs, waves, rows, 128), BF16),
+            pltpu.VMEM((levs * waves * rows, 128), F32),
             pltpu.VMEM((levs, slots) + legendre.shape[1:], BF16),
+            pltpu.SemaphoreType.DMA((6,)),
             pltpu.SemaphoreType.DMA,
             pltpu.SemaphoreType.DMA,
             pltpu.SemaphoreType.DMA((levs - 1,)),
             pltpu.SemaphoreType.DMA((levs - 1,)),
-            pltpu.SemaphoreType.DMA((2,)),
+            pltpu.SemaphoreType.DMA((levs - 1,)),
+            pltpu.SemaphoreType.DMA((levs - 1,)),
+            pltpu.SemaphoreType.DMA((3,)),
         ],
         compiler_params=pltpu.CompilerParams(
-            collective_id=0, has_side_effects=True, vmem_limit_bytes=40 * 2**20),
-    )(grid_adjoint, courant, row_points, wave_order, wave_order.reshape(1, -1), legendre,
-      vert_inverse)
+            collective_id=0, has_side_effects=True, vmem_limit_bytes=56 * 2**20),
+    )(grid_adjoint, courant, row_points, wave_order, orders, legendre, vert_inverse)
 
 
 def solution(mesh):

time: 30.8 us -> 22.7 us (0.74)
  Pallas kernels: 24.7 us -> 20.2 us
  local copies, waits for them, and re-layouts: 5.7 us -> 2.29 us
    pallas_call x1, Pallas kernels: 24.7 us -> 20.2 us  [body(): pl.pallas_call(functools.partial(kernel, waves, levs), out_shape=jax.Shap...]
    unnamed x13 -> x1, local copies, waits for them, and re-layouts: 5.7 us -> 2.29 us
where the time goes in v2:
time: 22.7 us; the launch traced here: 22.5 us
  Pallas kernels  20.2 us (89%)
  local copies, waits for them, and re-layouts  2.29 us (10%)
    pallas_call x1, Pallas kernels, body(): pl.pallas_call(functools.partial(kernel, waves, levs), out_shape=jax.Shap...  20.2 us
    unnamed x1, local copies, waits for them, and re-layouts  2.29 us

profile of v2, /device:TPU:1, one launch (start us, length us, event | category | flops | bytes accessed | tf_op | source)
XLA Modules:
  0.0 22.5 jit_solution(6044271838347141836)
XLA Ops:
  0.0 20.2 %shard_map.64 = f32[3,16,4,2,512]{4,3,2,1,0:T(2,128)} custom-call(bf16[3,4,4,1536]{3,2,1,0:T(4,128)(2,1)} %grid_hbm.1, bf16[4,4,1536]{2,1,0:T(4,128)(2,1)} %wind_hbm.1, s32[4]{0:T(128)} %points_hbm.1, s32[512]{0:T(512)} %order_hbm.1, s32[1,512]{1,0:T(1,128)} %bitcast.1, bf16[16,128,128]{2,1,0:T(8,128)(2,1)} %legendre_ref.1, f32[3,16,16]{2,1,0:T(8,128)} %vert_hbm.1), custom_call_target="tpu_custom_call" | custom-call | tf_op jit(solution)/shard_map/pallas_call | solution.py:269
  20.2 2.3 %copy.8 = f32[3,16,4,2,512]{4,3,2,1,0:T(2,128)} copy(f32[3,16,4,2,512]{4,3,2,1,0:T(2,128)} %shard_map.64) | data formatting | bytes 1572864

commit v3 on v2

--- a/solution.py
+++ b/solution.py
@@ -268,7 +268,7 @@
     hbm = pl.BlockSpec(memory_space=pltpu.HBM)
     return pl.pallas_call(
         functools.partial(kernel, waves, levs),
-        out_shape=jax.ShapeDtypeStruct((fields, levels * levs, slots, 2, degrees), F32),
+        out_shape=pltpu.VMEM((fields, levels * levs, slots, 2, degrees), F32),
         in_specs=[hbm] * 7,
         out_specs=pl.BlockSpec(memory_space=pltpu.VMEM),
         scratch_shapes=[

time: 22.7 us -> 20.3 us (0.89)
  local copies, waits for them, and re-layouts: 2.29 us -> 0.88 us
  Pallas kernels: 20.2 us -> 19.3 us
    unnamed x1, local copies, waits for them, and re-layouts: 2.29 us -> 0.88 us
    pallas_call x1, Pallas kernels: 20.2 us -> 19.3 us  [body(): pl.pallas_call(functools.partial(kernel, waves, levs), out_shape=pltpu.VM...]
where the time goes in v3:
time: 20.3 us; the launch traced here: 20.2 us
  Pallas kernels  19.3 us (95%)
  local copies, waits for them, and re-layouts  0.88 us (4%)
    pallas_call x1, Pallas kernels, body(): pl.pallas_call(functools.partial(kernel, waves, levs), out_shape=pltpu.VM...  19.3 us
    unnamed x1, local copies, waits for them, and re-layouts  0.88 us

profile of v3, /device:TPU:1, one launch (start us, length us, event | category | flops | bytes accessed | tf_op | source)
XLA Modules:
  0.0 20.2 jit_solution(17896346709979795049)
XLA Ops:
  0.0 19.3 %shard_map.64 = f32[3,16,4,2,512]{4,3,2,1,0:T(2,128)S(1)} custom-call(bf16[3,4,4,1536]{3,2,1,0:T(4,128)(2,1)} %grid_hbm.1, bf16[4,4,1536]{2,1,0:T(4,128)(2,1)} %wind_hbm.1, s32[4]{0:T(128)} %points_hbm.1, s32[512]{0:T(512)} %order_hbm.1, s32[1,512]{1,0:T(1,128)} %bitcast.1, bf16[16,128,128]{2,1,0:T(8,128)(2,1)} %legendre_ref.1, f32[3,16,16]{2,1,0:T(8,128)} %vert_hbm.1), custom_call_target="tpu_custom_call" | custom-call | tf_op jit(solution)/shard_map/pallas_call | solution.py:269
  19.3 0.9 %copy.8 = f32[3,16,4,2,512]{4,3,2,1,0:T(2,128)} copy(f32[3,16,4,2,512]{4,3,2,1,0:T(2,128)S(1)} %shard_map.64) | data formatting | bytes 1572864

commit v4 on v3

--- a/solution.py
+++ b/solution.py
@@ -78,27 +78,23 @@
     orders = orders_ref[...].astype(F32)
     high = jnp.floor(orders * 0.5)
     low = orders - 2.0 * high
-    pick = (iota((slots, slots), 0) == 4 * (iota((slots, slots), 1) % 128)
-            + iota((slots, slots), 1) // 128).astype(F32).astype(BF16)
+    column = iota((slots, slots), 1)
+    pick = (iota((slots, slots), 0) == 16 * (column % 32) + 4 * (column // 32 % 4)
+            + column // 128).astype(F32).astype(BF16)
     pair = jnp.concatenate([high, low, jnp.zeros((6, slots), F32)], axis=0).astype(BF16)
     moved = jnp.dot(pair, pick, preferred_element_type=F32)
     return 2.0 * moved[0:1] + moved[1:2]
 
 
-def row_transform(j, points_ref, orders, rows_ref, pages_ref):
-    blocks = rows_ref.shape[0]
+def row_tables(j, points_ref, orders, near_ref, far_ref):
     slots = orders.shape[1]
     count = jnp.full((1, slots), points_ref[j], jnp.int32).astype(F32)
     fine_cos, fine_sin = unit_circle(iota((16, 1), 0).astype(F32), orders, count)
     mid_cos, mid_sin = unit_circle(16.0 * iota((8, 1), 0).astype(F32), orders, count)
     far_cos, far_sin = unit_circle(128.0 * iota((16, 1), 0).astype(F32), orders, count)
     weight = jnp.where(2.0 * orders >= count, 0.0, jnp.where(orders == 0.0, 1.0, 2.0))
-    far_cos = far_cos * weight
-    far_sin = far_sin * weight
-    left = jnp.concatenate(
-        [rows_ref[k1, pl.ds(j, 16, stride=4), :] for k1 in range(blocks)], axis=0
-    ).astype(BF16)
-    stacked = []
+    far_ref[j, 0] = far_cos * weight
+    far_ref[j, 1] = far_sin * weight
     for i in range(slots // 128):
         own = slice(128 * i, 128 * (i + 1))
         c0, s0 = fine_cos[:, own], fine_sin[:, own]
@@ -107,16 +103,26 @@
             c1, s1 = mid_cos[b:b + 1, own], mid_sin[b:b + 1, own]
             real.append(c1 * c0 - s1 * s0)
             imag.append(c1 * s0 + s1 * c0)
-        table = jnp.concatenate(
+        near_ref[j, i] = jnp.concatenate(
             [jnp.concatenate(real, axis=0), jnp.concatenate(imag, axis=0)], axis=1
         ).astype(BF16)
-        partial = jnp.dot(left, table, preferred_element_type=F32)
+
+
+def row_transform(j, near_ref, far_ref, rows_ref, pages_ref):
+    blocks = rows_ref.shape[0]
+    left = jnp.concatenate(
+        [rows_ref[k1, pl.ds(j, 16, stride=4), :] for k1 in range(blocks)], axis=0
+    ).astype(BF16)
+    stacked = []
+    for i in range(near_ref.shape[1]):
+        own = slice(128 * i, 128 * (i + 1))
+        partial = jnp.dot(left, near_ref[j, i], preferred_element_type=F32)
         total_real = jnp.zeros((16, 128), F32)
         total_imag = jnp.zeros((16, 128), F32)
         for k1 in range(blocks):
             u = partial[16 * k1:16 * (k1 + 1), :128]
             v = partial[16 * k1:16 * (k1 + 1), 128:]
-            c2, s2 = far_cos[k1:k1 + 1, own], far_sin[k1:k1 + 1, own]
+            c2, s2 = far_ref[j, 0, k1:k1 + 1, own], far_ref[j, 1, k1:k1 + 1, own]
             total_real = total_real + (c2 * u - s2 * v)
             total_imag = total_imag + (c2 * v + s2 * u)
         stacked += [total_real, total_imag]
@@ -171,9 +177,9 @@
 
 def kernel(waves, levs, grid_hbm, wind_hbm, points_hbm, order_hbm, orders_hbm, legendre_ref,
            vert_hbm, out_ref, grid_ref, wind_ref, points_ref, order_ref, orders_ref, vert_ref,
-           rows_ref, pages_ref, send_ref, middle_ref, recv_ref, joined_ref, table_ref,
+           near_ref, far_ref, rows_ref, pages_ref, send_ref, middle_ref, recv_ref, joined_ref, table_ref,
            fetch_sem, wave_send_sem, wave_recv_sem, lev_send_sem, lev_recv_sem, table_send_sem,
-           table_recv_sem, local_sem):
+           table_recv_sem, local_sem, near_sem):
     w, v = lax.axis_index("wave"), lax.axis_index("lev")
     me = w * levs + v
     fetches = [
@@ -185,79 +191,119 @@
     for fetch in fetches:
         fetch.start()
     own_table = pltpu.make_async_copy(
-        legendre_ref.at[pl.ds(4 * v, 4)], table_ref.at[v], local_sem.at[0])
+        legendre_ref.at[pl.ds(4 * v, 4)], table_ref.at[v], local_sem.at[5])
     own_table.start()
 
+    planes, places = waves // 8, 8
+    plane, place = w // places, lax.rem(w, places)
+    mate = w + 1 - 2 * lax.rem(w, 2)
+    along_y = [places * plane + lax.rem(place + 2 * step, places) for step in range(1, 4)]
+
+    def others(first, last, action):
+        def one(step, carry):
+            target_plane = first + step // 6
+            target = places * target_plane + lax.rem(
+                2 * (place // 2) + 2 + lax.rem(step, 6), places)
+            action(target, target_plane)
+            return carry
+
+        lax.fori_loop(0, 6 * (last - first), one, 0)
+
     barrier = pltpu.get_barrier_semaphore()
+
+    def greet(target, lev):
+        pl.semaphore_signal(barrier, inc=1, device_id=(target, lev), device_id_type=MESH)
+
     for step in range(1, levs):
-        pl.semaphore_signal(barrier, inc=1, device_id=(w, lax.rem(v + step, levs)),
-                            device_id_type=MESH)
-
-    def greet(step, carry):
-        pl.semaphore_signal(barrier, inc=1, device_id=(lax.rem(w + step, waves), v),
-                            device_id_type=MESH)
-        return carry
-
-    lax.fori_loop(1, waves, greet, 0)
-    for fetch in fetches:
+        greet(w, lax.rem(v + step, levs))
+    for step in range(planes):
+        greet(lax.rem(mate + places * step, waves), v)
+        if step > 0:
+            greet(lax.rem(w + places * step, waves), v)
+    others(plane, plane + 1, lambda target, _: greet(target, v))
+    others(plane + 1, planes, lambda target, _: greet(target, v))
+    for fetch in fetches[2:5]:
         fetch.wait()
     orders = column_orders(orders_ref)
-    pl.semaphore_wait(barrier, waves - 1 + levs - 1)
-
+    for j in range(4):
+        row_tables(j, points_ref, orders, near_ref, far_ref)
+    fetches[0].wait()
+    fetches[1].wait()
+    advect(grid_ref, wind_ref, points_ref, rows_ref)
+    for j in range(4):
+        row_transform(j, near_ref, far_ref, rows_ref, pages_ref)
+    send_ref[...] = pages_ref[...].astype(BF16).reshape(send_ref.shape)
     table_copies = []
-    for step in (2, 1, 3):
+
+    def send_table(step, first, count):
         u = lax.rem(v + step, levs)
+        at = len(table_copies)
         copy = pltpu.make_async_remote_copy(
-            src_ref=legendre_ref.at[pl.ds(4 * u, 4)], dst_ref=table_ref.at[v],
-            send_sem=table_send_sem.at[step - 1], recv_sem=table_recv_sem.at[step - 1],
+            src_ref=legendre_ref.at[pl.ds(4 * u + first, count)],
+            dst_ref=table_ref.at[v, pl.ds(first, count)],
+            send_sem=table_send_sem.at[at], recv_sem=table_recv_sem.at[at],
             device_id=(w, u), device_id_type=MESH)
         copy.start()
         table_copies.append(copy)
 
-    advect(grid_ref, wind_ref, points_ref, rows_ref)
-    for j in range(4):
-        row_transform(j, points_ref, orders, rows_ref, pages_ref)
-    send_ref[...] = pages_ref[...].astype(BF16).reshape(send_ref.shape)
-
-    def send(step, carry):
-        target = lax.rem(w + step, waves)
+    own_pages = pltpu.make_async_copy(send_ref.at[:, w], middle_ref.at[:, w], local_sem.at[4])
+    own_pages.start()
+    pl.semaphore_wait(barrier, levs - 1 + 2 * planes - 1 + 6 + 6 * plane)
+    for target in along_y:
+        pl.semaphore_signal(near_sem, inc=1, device_id=(target, v), device_id_type=MESH)
+
+    def send(target, target_plane):
+        turn = lax.rem(target_plane + planes - plane, planes)
         pltpu.make_async_remote_copy(
-            src_ref=send_ref.at[target], dst_ref=middle_ref.at[:, w], send_sem=wave_send_sem,
-            recv_sem=wave_recv_sem, device_id=(target, v), device_id_type=MESH,
+            src_ref=send_ref.at[:, target], dst_ref=middle_ref.at[:, w],
+            send_sem=wave_send_sem, recv_sem=wave_recv_sem.at[turn],
+            device_id=(target, v), device_id_type=MESH,
         ).start()
-        return carry
-
-    lax.fori_loop(1, waves, send, 0)
-    own_pages = pltpu.make_async_copy(send_ref.at[w], middle_ref.at[:, w], local_sem.at[1])
-    own_pages.start()
+
+    others(0, plane, send)
+    for step in (2, 1, 3, 0):
+        target_plane = lax.rem(plane + step, planes)
+        send(lax.rem(mate + places * step, waves), target_plane)
+        if step > 0:
+            send(lax.rem(w + places * step, waves), target_plane)
+    others(plane, plane + 1, send)
+    send_table(1, 0, 4)
+    send_table(3, 0, 4)
+    pl.semaphore_wait(near_sem, len(along_y))
+    others(plane + 1, planes, send)
+    send_table(2, 0, 4)
+    fetches[5].wait()
     vert = vertical_table(vert_ref)
     own_pages.wait()
-    partner = {"device_id": (lax.rem(w + 1, waves), v), "device_id_type": MESH}
-    arrived = middle_ref.at[:, pl.ds(0, waves - 1)]
-    pltpu.make_async_remote_copy(
-        src_ref=arrived, dst_ref=arrived, send_sem=wave_send_sem, recv_sem=wave_recv_sem,
-        **partner).wait_recv()
-
-    lev_copies = []
-    for step in (2, 1, 3):
-        u = lax.rem(v + step, levs)
-        copy = pltpu.make_async_remote_copy(
-            src_ref=middle_ref.at[u], dst_ref=recv_ref.at[v],
-            send_sem=lev_send_sem.at[step - 1], recv_sem=lev_recv_sem.at[step - 1],
-            device_id=(w, u), device_id_type=MESH)
+    partner = {"device_id": (mate, v), "device_id_type": MESH}
+    lev_copies, own_blocks = [], []
+    for turn in (0, 1, 3, 2):
+        arrived = middle_ref.at[:, pl.ds(0, 7 if turn == 0 else 8)]
+        pltpu.make_async_remote_copy(
+            src_ref=arrived, dst_ref=arrived, send_sem=wave_send_sem,
+            recv_sem=wave_recv_sem.at[turn], **partner).wait_recv()
+        part = pl.ds(8 * lax.rem(plane + 4 - turn, 4), 8)
+        for step in (2, 1, 3):
+            u = lax.rem(v + step, levs)
+            at = 3 * turn + step - 1
+            copy = pltpu.make_async_remote_copy(
+                src_ref=middle_ref.at[u, part], dst_ref=recv_ref.at[v, part],
+                send_sem=lev_send_sem.at[at], recv_sem=lev_recv_sem.at[at],
+                device_id=(w, u), device_id_type=MESH)
+            copy.start()
+            lev_copies.append(copy)
+        copy = pltpu.make_async_copy(
+            middle_ref.at[v, part], recv_ref.at[v, part], local_sem.at[turn])
         copy.start()
-        lev_copies.append(copy)
-    own_block = pltpu.make_async_copy(middle_ref.at[v], recv_ref.at[v], local_sem.at[2])
-    own_block.start()
-    left = send_ref.at[pl.ds(0, waves - 1)]
-    pltpu.make_async_remote_copy(
-        src_ref=left, dst_ref=left, send_sem=wave_send_sem, recv_sem=wave_recv_sem,
-        **partner).wait_send()
-    own_block.wait()
+        own_blocks.append(copy)
     own_table.wait()
-    for copy in table_copies + lev_copies:
+    for copy in own_blocks + table_copies + lev_copies:
         copy.wait()
     finish(4 * me, order_ref, vert, recv_ref, joined_ref, table_ref, out_ref)
+    left = send_ref.at[:, pl.ds(0, waves - 1)]
+    pltpu.make_async_remote_copy(
+        src_ref=left, dst_ref=left, send_sem=wave_send_sem, recv_sem=wave_recv_sem.at[0],
+        **partner).wait_send()
 
 
 def body(grid_adjoint, courant, row_points, wave_order, legendre, vert_inverse, *, waves, levs):
@@ -278,21 +324,24 @@
             pltpu.SMEM(wave_order.shape, jnp.int32),
             pltpu.VMEM(orders.shape, jnp.int32),
             pltpu.VMEM(vert_inverse.shape, F32),
+            pltpu.VMEM((rows, 4, 128, 256), BF16),
+            pltpu.VMEM((rows, 2, 16, 512), F32),
             pltpu.VMEM((width // 128, 64, 128), F32),
             pltpu.VMEM((waves * levs, rows, 128), F32),
-            pltpu.VMEM((waves, levs, rows, 128), BF16),
+            pltpu.VMEM((levs, waves, rows, 128), BF16),
             pltpu.VMEM((levs, waves, rows, 128), BF16),
             pltpu.VMEM((levs, waves, rows, 128), BF16),
             pltpu.VMEM((levs * waves * rows, 128), F32),
             pltpu.VMEM((levs, slots) + legendre.shape[1:], BF16),
             pltpu.SemaphoreType.DMA((6,)),
             pltpu.SemaphoreType.DMA,
-            pltpu.SemaphoreType.DMA,
-            pltpu.SemaphoreType.DMA((levs - 1,)),
-            pltpu.SemaphoreType.DMA((levs - 1,)),
-            pltpu.SemaphoreType.DMA((levs - 1,)),
-            pltpu.SemaphoreType.DMA((levs - 1,)),
-            pltpu.SemaphoreType.DMA((3,)),
+            pltpu.SemaphoreType.DMA((4,)),
+            pltpu.SemaphoreType.DMA((12,)),
+            pltpu.SemaphoreType.DMA((12,)),
+            pltpu.SemaphoreType.DMA((8,)),
+            pltpu.SemaphoreType.DMA((8,)),
+            pltpu.SemaphoreType.DMA((6,)),
+            pltpu.SemaphoreType.REGULAR,
         ],
         compiler_params=pltpu.CompilerParams(
             collective_id=0, has_side_effects=True, vmem_limit_bytes=56 * 2**20),

time: 20.3 us -> 19 us (0.936)
  Pallas kernels: 19.3 us -> 18 us
    pallas_call x1, Pallas kernels: 19.3 us -> 18 us  [body(): pl.pallas_call(functools.partial(kernel, waves, levs), out_shape=pltpu.VM...]
where the time goes in v4:
time: 19 us; the launch traced here: 18.9 us
  Pallas kernels  18 us (95%)
  local copies, waits for them, and re-layouts  0.88 us (5%)
    pallas_call x1, Pallas kernels, body(): pl.pallas_call(functools.partial(kernel, waves, levs), out_shape=pltpu.VM...  18 us
    unnamed x1, local copies, waits for them, and re-layouts  0.88 us

profile of v4, /device:TPU:1, one launch (start us, length us, event | category | flops | bytes accessed | tf_op | source)
XLA Modules:
  0.0 18.9 jit_solution(10435274378584505180)
XLA Ops:
  0.0 18.0 %shard_map.64 = f32[3,16,4,2,512]{4,3,2,1,0:T(2,128)S(1)} custom-call(bf16[3,4,4,1536]{3,2,1,0:T(4,128)(2,1)} %grid_hbm.1, bf16[4,4,1536]{2,1,0:T(4,128)(2,1)} %wind_hbm.1, s32[4]{0:T(128)} %points_hbm.1, s32[512]{0:T(512)} %order_hbm.1, s32[1,512]{1,0:T(1,128)} %bitcast.1, bf16[16,128,128]{2,1,0:T(8,128)(2,1)} %legendre_ref.1, f32[3,16,16]{2,1,0:T(8,128)} %vert_hbm.1), custom_call_target="tpu_custom_call" | custom-call | tf_op jit(solution)/shard_map/pallas_call | solution.py:315
  18.0 0.9 %copy.8 = f32[3,16,4,2,512]{4,3,2,1,0:T(2,128)} copy(f32[3,16,4,2,512]{4,3,2,1,0:T(2,128)S(1)} %shard_map.64) | data formatting | bytes 1572864

commit v5 on v4

--- a/solution.py
+++ b/solution.py
@@ -73,16 +73,13 @@
     rows_ref[:, used:, :] = jnp.zeros((rows_ref.shape[0], rows_ref.shape[1] - used, 128), F32)
 
 
-def column_orders(orders_ref):
+def column_orders(orders_ref, pick_ref):
     slots = orders_ref.shape[1]
     orders = orders_ref[...].astype(F32)
     high = jnp.floor(orders * 0.5)
     low = orders - 2.0 * high
-    column = iota((slots, slots), 1)
-    pick = (iota((slots, slots), 0) == 16 * (column % 32) + 4 * (column // 32 % 4)
-            + column // 128).astype(F32).astype(BF16)
     pair = jnp.concatenate([high, low, jnp.zeros((6, slots), F32)], axis=0).astype(BF16)
-    moved = jnp.dot(pair, pick, preferred_element_type=F32)
+    moved = jnp.dot(pair, pick_ref[...], preferred_element_type=F32)
     return 2.0 * moved[0:1] + moved[1:2]
 
 
@@ -146,19 +143,17 @@
     return jnp.concatenate([jnp.where(slot == i, block, 0.0) for i in range(4)], axis=0)
 
 
-def finish(first_slot, order_ref, vert, pages_ref, joined_ref, table_ref, out_ref):
-    levs, waves, rows, _ = pages_ref.shape
-    for s in range(levs * waves):
-        joined_ref[rows * s:rows * (s + 1), :] = pages_ref[s // waves, s % waves].astype(F32)
+def finish(first_slot, order_ref, vert, joined_ref, table_ref, out_ref):
     high = vert.astype(BF16)
     low = (vert - high.astype(F32)).astype(BF16)
     mixed = None
     for v in range(4):
         block = joined_ref[128 * v:128 * (v + 1), :].astype(BF16)
         own = slice(128 * v, 128 * (v + 1))
-        for part in (high, low):
-            term = lax.dot_general(part[:, own], block, NT, preferred_element_type=F32)
-            mixed = term if mixed is None else mixed + term
+        term = lax.dot_general(
+            jnp.concatenate([high[:, own], low[:, own]], axis=1),
+            jnp.concatenate([block, block], axis=1), NT, preferred_element_type=F32)
+        mixed = term if mixed is None else mixed + term
     mixed_high = mixed.astype(BF16)
     mixed_low = (mixed - mixed_high.astype(F32)).astype(BF16)
     both = jnp.concatenate([mixed_high, mixed_low], axis=1)
@@ -177,7 +172,8 @@
 
 def kernel(waves, levs, grid_hbm, wind_hbm, points_hbm, order_hbm, orders_hbm, legendre_ref,
            vert_hbm, out_ref, grid_ref, wind_ref, points_ref, order_ref, orders_ref, vert_ref,
-           near_ref, far_ref, rows_ref, pages_ref, send_ref, middle_ref, recv_ref, joined_ref, table_ref,
+           pick_ref, near_ref, far_ref, rows_ref, pages_ref, send_ref, middle_ref, recv_ref,
+           joined_ref, table_ref,
            fetch_sem, wave_send_sem, wave_recv_sem, lev_send_sem, lev_recv_sem, table_send_sem,
            table_recv_sem, local_sem, near_sem):
     w, v = lax.axis_index("wave"), lax.axis_index("lev")
@@ -185,8 +181,8 @@
     fetches = [
         pltpu.make_async_copy(source, target, fetch_sem.at[at])
         for at, (source, target) in enumerate((
-            (grid_hbm, grid_ref), (wind_hbm, wind_ref), (points_hbm, points_ref),
-            (order_hbm, order_ref), (orders_hbm, orders_ref), (vert_hbm, vert_ref)))
+            (orders_hbm, orders_ref), (points_hbm, points_ref), (wind_hbm, wind_ref),
+            (grid_hbm, grid_ref), (order_hbm, order_ref), (vert_hbm, vert_ref)))
     ]
     for fetch in fetches:
         fetch.start()
@@ -222,13 +218,17 @@
             greet(lax.rem(w + places * step, waves), v)
     others(plane, plane + 1, lambda target, _: greet(target, v))
     others(plane + 1, planes, lambda target, _: greet(target, v))
-    for fetch in fetches[2:5]:
-        fetch.wait()
-    orders = column_orders(orders_ref)
+    order_count = orders_ref.shape[1]
+    column = iota((order_count, order_count), 1)
+    pick_ref[...] = (iota((order_count, order_count), 0) == 16 * (column % 32) + 4 * (column // 32 % 4)
+            + column // 128).astype(F32).astype(BF16)
+    fetches[0].wait()
+    fetches[1].wait()
+    orders = column_orders(orders_ref, pick_ref)
     for j in range(4):
         row_tables(j, points_ref, orders, near_ref, far_ref)
-    fetches[0].wait()
-    fetches[1].wait()
+    fetches[2].wait()
+    fetches[3].wait()
     advect(grid_ref, wind_ref, points_ref, rows_ref)
     for j in range(4):
         row_transform(j, near_ref, far_ref, rows_ref, pages_ref)
@@ -246,7 +246,7 @@
         copy.start()
         table_copies.append(copy)
 
-    own_pages = pltpu.make_async_copy(send_ref.at[:, w], middle_ref.at[:, w], local_sem.at[4])
+    own_pages = pltpu.make_async_copy(send_ref.at[:, w], middle_ref.at[:, w], wave_recv_sem.at[0])
     own_pages.start()
     pl.semaphore_wait(barrier, levs - 1 + 2 * planes - 1 + 6 + 6 * plane)
     for target in along_y:
@@ -272,20 +272,21 @@
     pl.semaphore_wait(near_sem, len(along_y))
     others(plane + 1, planes, send)
     send_table(2, 0, 4)
+    fetches[4].wait()
     fetches[5].wait()
     vert = vertical_table(vert_ref)
-    own_pages.wait()
     partner = {"device_id": (mate, v), "device_id_type": MESH}
     lev_copies, own_blocks = [], []
-    for turn in (0, 1, 3, 2):
-        arrived = middle_ref.at[:, pl.ds(0, 7 if turn == 0 else 8)]
+    arrived = middle_ref.at[:, pl.ds(0, places)]
+    for source in range(planes):
+        turn = lax.rem(plane + planes - source, planes)
         pltpu.make_async_remote_copy(
             src_ref=arrived, dst_ref=arrived, send_sem=wave_send_sem,
             recv_sem=wave_recv_sem.at[turn], **partner).wait_recv()
-        part = pl.ds(8 * lax.rem(plane + 4 - turn, 4), 8)
+        part = pl.ds(places * source, places)
         for step in (2, 1, 3):
             u = lax.rem(v + step, levs)
-            at = 3 * turn + step - 1
+            at = 3 * source + step - 1
             copy = pltpu.make_async_remote_copy(
                 src_ref=middle_ref.at[u, part], dst_ref=recv_ref.at[v, part],
                 send_sem=lev_send_sem.at[at], recv_sem=lev_recv_sem.at[at],
@@ -293,13 +294,23 @@
             copy.start()
             lev_copies.append(copy)
         copy = pltpu.make_async_copy(
-            middle_ref.at[v, part], recv_ref.at[v, part], local_sem.at[turn])
+            middle_ref.at[v, part], recv_ref.at[v, part], local_sem.at[source])
         copy.start()
         own_blocks.append(copy)
     own_table.wait()
-    for copy in own_blocks + table_copies + lev_copies:
-        copy.wait()
-    finish(4 * me, order_ref, vert, recv_ref, joined_ref, table_ref, out_ref)
+    for copy in table_copies:
+        copy.wait_recv()
+    for source in range(planes):
+        for copy in lev_copies[3 * source:3 * source + 3]:
+            copy.wait_recv()
+        own_blocks[source].wait()
+        for lev in range(levs):
+            for at in range(places):
+                row = 4 * (waves * lev + places * source + at)
+                joined_ref[row:row + 4, :] = recv_ref[lev, places * source + at].astype(F32)
+    finish(4 * me, order_ref, vert, joined_ref, table_ref, out_ref)
+    for copy in table_copies + lev_copies:
+        copy.wait_send()
     left = send_ref.at[:, pl.ds(0, waves - 1)]
     pltpu.make_async_remote_copy(
         src_ref=left, dst_ref=left, send_sem=wave_send_sem, recv_sem=wave_recv_sem.at[0],
@@ -324,6 +335,7 @@
             pltpu.SMEM(wave_order.shape, jnp.int32),
             pltpu.VMEM(orders.shape, jnp.int32),
             pltpu.VMEM(vert_inverse.shape, F32),
+            pltpu.VMEM((512, 512), BF16),
             pltpu.VMEM((rows, 4, 128, 256), BF16),
             pltpu.VMEM((rows, 2, 16, 512), F32),
             pltpu.VMEM((width // 128, 64, 128), F32),

time: 19 us -> 18.6 us (0.979)
  Pallas kernels: 18 us -> 17.6 us
    pallas_call x1, Pallas kernels: 18 us -> 17.6 us  [body(): pl.pallas_call(functools.partial(kernel, waves, levs), out_shape=pltpu.VM...]
where the time goes in v5:
time: 18.6 us; the launch traced here: 18.4 us
  Pallas kernels  17.6 us (95%)
  local copies, waits for them, and re-layouts  0.88 us (5%)
    pallas_call x1, Pallas kernels, body(): pl.pallas_call(functools.partial(kernel, waves, levs), out_shape=pltpu.VM...  17.6 us
    unnamed x1, local copies, waits for them, and re-layouts  0.88 us

profile of v5, /device:TPU:1, one launch (start us, length us, event | category | flops | bytes accessed | tf_op | source)
XLA Modules:
  0.0 18.4 jit_solution(2266486005625171879)
XLA Ops:
  0.0 17.6 %shard_map.64 = f32[3,16,4,2,512]{4,3,2,1,0:T(2,128)S(1)} custom-call(bf16[3,4,4,1536]{3,2,1,0:T(4,128)(2,1)} %grid_hbm.1, bf16[4,4,1536]{2,1,0:T(4,128)(2,1)} %wind_hbm.1, s32[4]{0:T(128)} %points_hbm.1, s32[512]{0:T(512)} %order_hbm.1, s32[1,512]{1,0:T(1,128)} %bitcast.1, bf16[16,128,128]{2,1,0:T(8,128)(2,1)} %legendre_ref.1, f32[3,16,16]{2,1,0:T(8,128)} %vert_hbm.1), custom_call_target="tpu_custom_call" | custom-call | tf_op jit(solution)/shard_map/pallas_call | solution.py:326
  17.6 0.9 %copy.8 = f32[3,16,4,2,512]{4,3,2,1,0:T(2,128)} copy(f32[3,16,4,2,512]{4,3,2,1,0:T(2,128)S(1)} %shard_map.64) | data formatting | bytes 1572864

commit v6 on v5

--- a/solution.py
+++ b/solution.py
@@ -86,9 +86,19 @@
 def row_tables(j, points_ref, orders, near_ref, far_ref):
     slots = orders.shape[1]
     count = jnp.full((1, slots), points_ref[j], jnp.int32).astype(F32)
-    fine_cos, fine_sin = unit_circle(iota((16, 1), 0).astype(F32), orders, count)
-    mid_cos, mid_sin = unit_circle(16.0 * iota((8, 1), 0).astype(F32), orders, count)
-    far_cos, far_sin = unit_circle(128.0 * iota((16, 1), 0).astype(F32), orders, count)
+    row = iota((8, 1), 0)
+    low_cos, low_sin = unit_circle(row.astype(F32), orders, count)
+    mid_cos, mid_sin = unit_circle(16.0 * row.astype(F32), orders, count)
+    far_cos, far_sin = unit_circle(128.0 * row.astype(F32), orders, count)
+    step_cos, step_sin = unit_circle(jnp.where(row == 0, 8, 1024).astype(F32), orders, count)
+
+    def twice(c, s, at):
+        c1, s1 = step_cos[at:at + 1], step_sin[at:at + 1]
+        return (jnp.concatenate([c, c * c1 - s * s1], axis=0),
+                jnp.concatenate([s, c * s1 + s * c1], axis=0))
+
+    fine_cos, fine_sin = twice(low_cos, low_sin, 0)
+    far_cos, far_sin = twice(far_cos, far_sin, 1)
     weight = jnp.where(2.0 * orders >= count, 0.0, jnp.where(orders == 0.0, 1.0, 2.0))
     far_ref[j, 0] = far_cos * weight
     far_ref[j, 1] = far_sin * weight
@@ -132,37 +142,30 @@
     rows = jnp.concatenate(
         [lax.dot_general(spread, vert_ref[f], NT, precision=lax.Precision.HIGHEST,
                          preferred_element_type=F32) for f in range(fields)], axis=0)
-    column = iota((levels, 512), 1)
-    pick = (iota((levels, 512), 0) == 4 * (column // 128) + column % 4).astype(F32)
+    column = iota((levels, 128), 1)
+    pick = (iota((levels, 128), 0) == 4 * (column // 32) + column % 4).astype(F32)
     block = jnp.dot(rows, pick, precision=lax.Precision.HIGHEST, preferred_element_type=F32)
     shape = block.shape
     row, column = iota(shape, 0), iota(shape, 1)
     keep = (row // (2 * levels) == column // 4 % 4) & (row % 2 == column // 16 % 2)
-    block = jnp.where(keep, block, 0.0)
-    slot = column // 32 % 4
-    return jnp.concatenate([jnp.where(slot == i, block, 0.0) for i in range(4)], axis=0)
+    return jnp.where(keep, block, 0.0)
 
 
 def finish(first_slot, order_ref, vert, joined_ref, table_ref, out_ref):
     high = vert.astype(BF16)
     low = (vert - high.astype(F32)).astype(BF16)
-    mixed = None
-    for v in range(4):
-        block = joined_ref[128 * v:128 * (v + 1), :].astype(BF16)
-        own = slice(128 * v, 128 * (v + 1))
-        term = lax.dot_general(
-            jnp.concatenate([high[:, own], low[:, own]], axis=1),
-            jnp.concatenate([block, block], axis=1), NT, preferred_element_type=F32)
-        mixed = term if mixed is None else mixed + term
-    mixed_high = mixed.astype(BF16)
-    mixed_low = (mixed - mixed_high.astype(F32)).astype(BF16)
-    both = jnp.concatenate([mixed_high, mixed_low], axis=1)
+    halves = jnp.concatenate([high, low], axis=1)
     fields, levels = out_ref.shape[0], out_ref.shape[1]
-    lines = fields * levels * 2
     for i in range(4):
+        block = joined_ref[i].astype(BF16)
+        mixed = lax.dot_general(halves, jnp.concatenate([block, block], axis=1), NT,
+                                preferred_element_type=F32)
+        mixed_high = mixed.astype(BF16)
+        mixed_low = (mixed - mixed_high.astype(F32)).astype(BF16)
+        both = jnp.concatenate([mixed_high, mixed_low], axis=1)
         table = jnp.concatenate([table_ref[v, i] for v in range(4)], axis=0)
         table = jnp.concatenate([table, table], axis=1)
-        summed = lax.dot_general(both[lines * i:lines * (i + 1)], table, NT,
+        summed = lax.dot_general(both, table, NT,
                                  preferred_element_type=F32)
         degree = iota(summed.shape, 1)
         summed = jnp.where(degree >= order_ref[first_slot + i], summed, 0.0)
@@ -173,7 +176,7 @@
 def kernel(waves, levs, grid_hbm, wind_hbm, points_hbm, order_hbm, orders_hbm, legendre_ref,
            vert_hbm, out_ref, grid_ref, wind_ref, points_ref, order_ref, orders_ref, vert_ref,
            pick_ref, near_ref, far_ref, rows_ref, pages_ref, send_ref, middle_ref, recv_ref,
-           joined_ref, table_ref,
+           chunk_ref, joined_ref, table_ref,
            fetch_sem, wave_send_sem, wave_recv_sem, lev_send_sem, lev_recv_sem, table_send_sem,
            table_recv_sem, local_sem, near_sem):
     w, v = lax.axis_index("wave"), lax.axis_index("lev")
@@ -205,6 +208,8 @@
 
         lax.fori_loop(0, 6 * (last - first), one, 0)
 
+    greeted = plane - plane // 3
+    last = plane + 1 + (3 - plane) // 2 * (planes - 1 - plane)
     barrier = pltpu.get_barrier_semaphore()
 
     def greet(target, lev):
@@ -217,7 +222,7 @@
         if step > 0:
             greet(lax.rem(w + places * step, waves), v)
     others(plane, plane + 1, lambda target, _: greet(target, v))
-    others(plane + 1, planes, lambda target, _: greet(target, v))
+    others(plane + 1, last, lambda target, _: greet(target, v))
     order_count = orders_ref.shape[1]
     column = iota((order_count, order_count), 1)
     pick_ref[...] = (iota((order_count, order_count), 0) == 16 * (column % 32) + 4 * (column // 32 % 4)
@@ -248,7 +253,7 @@
 
     own_pages = pltpu.make_async_copy(send_ref.at[:, w], middle_ref.at[:, w], wave_recv_sem.at[0])
     own_pages.start()
-    pl.semaphore_wait(barrier, levs - 1 + 2 * planes - 1 + 6 + 6 * plane)
+    pl.semaphore_wait(barrier, levs - 1 + 2 * planes - 1 + 6 + 6 * greeted)
     for target in along_y:
         pl.semaphore_signal(near_sem, inc=1, device_id=(target, v), device_id_type=MESH)
 
@@ -260,7 +265,7 @@
             device_id=(target, v), device_id_type=MESH,
         ).start()
 
-    others(0, plane, send)
+    others(0, greeted, send)
     for step in (2, 1, 3, 0):
         target_plane = lax.rem(plane + step, planes)
         send(lax.rem(mate + places * step, waves), target_plane)
@@ -270,6 +275,7 @@
     send_table(1, 0, 4)
     send_table(3, 0, 4)
     pl.semaphore_wait(near_sem, len(along_y))
+    others(greeted, plane, send)
     others(plane + 1, planes, send)
     send_table(2, 0, 4)
     fetches[4].wait()
@@ -304,10 +310,15 @@
         for copy in lev_copies[3 * source:3 * source + 3]:
             copy.wait_recv()
         own_blocks[source].wait()
+        chunks = []
         for lev in range(levs):
             for at in range(places):
-                row = 4 * (waves * lev + places * source + at)
-                joined_ref[row:row + 4, :] = recv_ref[lev, places * source + at].astype(F32)
+                row = 4 * (places * lev + at)
+                chunk_ref[row:row + 4, :] = recv_ref[lev, places * source + at].astype(F32)
+            chunks.append(chunk_ref[4 * places * lev:4 * places * (lev + 1), :])
+        for i in range(4):
+            joined_ref[i, 4 * places * source:4 * places * (source + 1), :] = jnp.concatenate(
+                [chunk[:, 32 * i:32 * (i + 1)] for chunk in chunks], axis=1)
     finish(4 * me, order_ref, vert, joined_ref, table_ref, out_ref)
     for copy in table_copies + lev_copies:
         copy.wait_send()
@@ -343,7 +354,8 @@
             pltpu.VMEM((levs, waves, rows, 128), BF16),
             pltpu.VMEM((levs, waves, rows, 128), BF16),
             pltpu.VMEM((levs, waves, rows, 128), BF16),
-            pltpu.VMEM((levs * waves * rows, 128), F32),
+            pltpu.VMEM((levs * 8 * rows, 128), F32),
+            pltpu.VMEM((slots, waves * rows, 128), F32),
             pltpu.VMEM((levs, slots) + legendre.shape[1:], BF16),
             pltpu.SemaphoreType.DMA((6,)),
             pltpu.SemaphoreType.DMA,

time: 18.6 us -> 18.4 us (0.989)
  Pallas kernels: 17.6 us -> 17.4 us
where the time goes in v6:
time: 18.4 us; the launch traced here: 18.3 us
  Pallas kernels  17.4 us (95%)
  local copies, waits for them, and re-layouts  0.88 us (5%)
    pallas_call x1, Pallas kernels, body(): pl.pallas_call(functools.partial(kernel, waves, levs), out_shape=pltpu.VM...  17.4 us
    unnamed x1, local copies, waits for them, and re-layouts  0.88 us

profile of v6, /device:TPU:1, one launch (start us, length us, event | category | flops | bytes accessed | tf_op | source)
XLA Modules:
  0.0 18.3 jit_solution(1145604532329948756)
XLA Ops:
  0.0 17.4 %shard_map.64 = f32[3,16,4,2,512]{4,3,2,1,0:T(2,128)S(1)} custom-call(bf16[3,4,4,1536]{3,2,1,0:T(4,128)(2,1)} %grid_hbm.1, bf16[4,4,1536]{2,1,0:T(4,128)(2,1)} %wind_hbm.1, s32[4]{0:T(128)} %points_hbm.1, s32[512]{0:T(512)} %order_hbm.1, s32[1,512]{1,0:T(1,128)} %bitcast.1, bf16[16,128,128]{2,1,0:T(8,128)(2,1)} %legendre_ref.1, f32[3,16,16]{2,1,0:T(8,128)} %vert_hbm.1), custom_call_target="tpu_custom_call" | custom-call | tf_op jit(solution)/shard_map/pallas_call | solution.py:337
  17.4 0.9 %copy.8 = f32[3,16,4,2,512]{4,3,2,1,0:T(2,128)} copy(f32[3,16,4,2,512]{4,3,2,1,0:T(2,128)S(1)} %shard_map.64) | data formatting | bytes 1572864

commit v7 on v6

--- a/solution.py
+++ b/solution.py
@@ -156,13 +156,15 @@
     low = (vert - high.astype(F32)).astype(BF16)
     halves = jnp.concatenate([high, low], axis=1)
     fields, levels = out_ref.shape[0], out_ref.shape[1]
-    for i in range(4):
-        block = joined_ref[i].astype(BF16)
-        mixed = lax.dot_general(halves, jnp.concatenate([block, block], axis=1), NT,
-                                preferred_element_type=F32)
-        mixed_high = mixed.astype(BF16)
-        mixed_low = (mixed - mixed_high.astype(F32)).astype(BF16)
-        both = jnp.concatenate([mixed_high, mixed_low], axis=1)
+    slots, rows, width = joined_ref.shape
+    block = joined_ref[...].reshape(slots * rows, width).astype(BF16)
+    mixed = lax.dot_general(halves, jnp.concatenate([block, block], axis=1), NT,
+                            preferred_element_type=F32)
+    mixed_high = mixed.astype(BF16)
+    mixed_low = (mixed - mixed_high.astype(F32)).astype(BF16)
+    for i in range(slots):
+        own = slice(rows * i, rows * (i + 1))
+        both = jnp.concatenate([mixed_high[:, own], mixed_low[:, own]], axis=1)
         table = jnp.concatenate([table_ref[v, i] for v in range(4)], axis=0)
         table = jnp.concatenate([table, table], axis=1)
         summed = lax.dot_general(both, table, NT,

time: 18.4 us -> 18.2 us (0.989)
  Pallas kernels: 17.4 us -> 17.2 us
    pallas_call x1, Pallas kernels: 17.4 us -> 17.2 us  [body(): pl.pallas_call(functools.partial(kernel, waves, levs), out_shape=pltpu.VM...]
where the time goes in v7:
time: 18.2 us; the launch traced here: 18.1 us
  Pallas kernels  17.2 us (95%)
  local copies, waits for them, and re-layouts  0.88 us (5%)
    pallas_call x1, Pallas kernels, body(): pl.pallas_call(functools.partial(kernel, waves, levs), out_shape=pltpu.VM...  17.2 us
    unnamed x1, local copies, waits for them, and re-layouts  0.88 us

profile of v7, /device:TPU:1, one launch (start us, length us, event | category | flops | bytes accessed | tf_op | source)
XLA Modules:
  0.0 18.1 jit_solution(1972462742547914523)
XLA Ops:
  0.0 17.2 %shard_map.64 = f32[3,16,4,2,512]{4,3,2,1,0:T(2,128)S(1)} custom-call(bf16[3,4,4,1536]{3,2,1,0:T(4,128)(2,1)} %grid_hbm.1, bf16[4,4,1536]{2,1,0:T(4,128)(2,1)} %wind_hbm.1, s32[4]{0:T(128)} %points_hbm.1, s32[512]{0:T(512)} %order_hbm.1, s32[1,512]{1,0:T(1,128)} %bitcast.1, bf16[16,128,128]{2,1,0:T(8,128)(2,1)} %legendre_ref.1, f32[3,16,16]{2,1,0:T(8,128)} %vert_hbm.1), custom_call_target="tpu_custom_call" | custom-call | tf_op jit(solution)/shard_map/pallas_call | solution.py:339
  17.2 0.9 %copy.8 = f32[3,16,4,2,512]{4,3,2,1,0:T(2,128)} copy(f32[3,16,4,2,512]{4,3,2,1,0:T(2,128)S(1)} %shard_map.64) | data formatting | bytes 1572864
